TPU v7x, 1024 devices: a whole 4x4x32 slice. The times are simulated.
1024 devices in a mesh: lon: 32 (over z_lo, x), lat: 32 (over y, z_hi, core).
Axes of the slice: x: 4, y: 4, z: 32 (z_hi: 4, z_lo: 8; z = z_hi * 8 + z_lo), core: 2. Of those that a mesh axis runs over, the one named last changes fastest.
Arguments:
- model_variables: float32 [3, 64, 256, 4096], P(None, None, 'lat', 'lon'), may hold values from -6 to 6
- obs_cell: int32 [2, 64], replicated, may hold values from 0 to 1048575
- obs_value: float32 [2, 64], replicated, may hold values from -8 to 8
- obs_variance: float32 [2, 64], replicated, may hold values from 0.2 to 2
- tile_mask: int32 [2, 64, 1024], P(None, None, ('lon', 'lat')), may hold values 0 or 1
Outputs:
- analysis: float32 [3, 64, 256, 4096], P(None, None, 'lat', 'lon')
All inputs are finite; a program needn't handle non-finite values. No bound on the sum of `tile_mask` on one device may be relied on, other than what follows from the above.
Results may differ from a plain program's by a relative error of at most 0.00015.
Values sent between devices are 32-bit elements; how exact they have to be, the bound alone decides.
A program may use at most 32 MiB of HBM per device.

v0:
```python
import jax
import jax.numpy as jnp
from jax import lax
from jax.sharding import PartitionSpec as P

STEPS = 4
NBATCH = 2
LOC_RADIUS = 256


CORIOLIS = 0.1
COURANT = 0.5
SMALL_EPSILON = 1e-06


def with_halo(cells, sides, width):
    for axis, dim in sides:
        count = lax.axis_size(axis)
        head = lax.slice_in_dim(cells, 0, width, axis=dim)
        tail = lax.slice_in_dim(cells, cells.shape[dim] - width, cells.shape[dim], axis=dim)
        cells = jnp.concatenate(
            [
                lax.ppermute(tail, axis, [(i, (i + 1) % count) for i in range(count)]),
                cells,
                lax.ppermute(head, axis, [((i + 1) % count, i) for i in range(count)]),
            ],
            axis=dim,
        )
    return cells


def increments(prior, value, variance, ensemble_snapshots):
    center = jnp.mean(prior)
    spread_dev = prior - center
    spread = jnp.sum(spread_dev * spread_dev) / (ensemble_snapshots - 1) + SMALL_EPSILON
    post = 1.0 / (1.0 / spread + 1.0 / variance)
    post_mean = post * (center / spread + value / variance)
    delta = post_mean - center + (jnp.sqrt(post / spread) - 1.0) * spread_dev
    slope = spread_dev / ((ensemble_snapshots - 1) * spread)
    return (delta, slope)


def inside_rows(count, first, total_rows):
    global_rows = first + jnp.arange(count, dtype=jnp.int32)
    return ((global_rows >= 0) & (global_rows < total_rows))[:, None]


def coriolis_rows(count, first, total_rows):
    rows = (first + jnp.arange(count, dtype=jnp.int32)).astype(jnp.float32)
    return (CORIOLIS * ((2.0 * rows + 1.0) / total_rows - 1.0))[:, None]


def body(model_variables, obs_cell, obs_value, obs_variance, tile_mask):
    ensemble_snapshots = model_variables.shape[1]
    rows_dev = model_variables.shape[2]
    cols_dev = model_variables.shape[3]
    latitude_index = lax.axis_index("lat")
    lon_index = lax.axis_index("lon")
    total_rows = rows_dev * lax.axis_size("lat")
    total_cols = cols_dev * lax.axis_size("lon")
    row_first = latitude_index * rows_dev
    col_first = lon_index * cols_dev
    inside = inside_rows(rows_dev + 2, row_first - 1, total_rows)
    coriolis = coriolis_rows(rows_dev, row_first, total_rows)
    surface_elevation, east, north = (model_variables[0], model_variables[1], model_variables[2])
    for step in range(STEPS):
        flows = with_halo(jnp.stack([east, north]), (("lon", 3), ("lat", 2)), 1)
        flows = jnp.where(inside, flows, 0.0)
        east_grad = 0.5 * (flows[0, :, 1:-1, 2:] - flows[0, :, 1:-1, :-2])
        meridional_slope = 0.5 * (flows[1, :, 2:, 1:-1] - flows[1, :, :-2, 1:-1])
        surface_elevation = surface_elevation - COURANT * (east_grad + meridional_slope)
        widened = with_halo(surface_elevation, (("lon", 2), ("lat", 1)), 1)
        widened = jnp.where(inside, widened, 0.0)
        east_next = (
            east
            + coriolis * north
            - COURANT * (0.5 * (widened[:, 1:-1, 2:] - widened[:, 1:-1, :-2]))
        )
        north = (
            north
            - coriolis * east
            - COURANT * (0.5 * (widened[:, 2:, 1:-1] - widened[:, :-2, 1:-1]))
        )
        east = east_next
    layered_arrays = jnp.stack([surface_elevation, east, north])
    centre_lat = row_first + rows_dev // 2
    central_longitude = col_first + cols_dev // 2
    for batch in range(NBATCH):
        cells = obs_cell[batch]
        obs_lat = cells // total_cols
        obs_lon = cells % total_cols
        lat_gap = obs_lat - centre_lat
        lon_gap = jnp.abs(obs_lon - central_longitude)
        lon_gap = jnp.minimum(lon_gap, total_cols - lon_gap)
        distance = (lat_gap * lat_gap + lon_gap * lon_gap).astype(jnp.float32)
        weights = tile_mask[batch][:, 0].astype(jnp.float32) / (
            1.0 + distance / (LOC_RADIUS * LOC_RADIUS)
        )
        local_lat = cells // total_cols - row_first
        local_lon = cells % total_cols - col_first
        owned = (
            (local_lat >= 0) & (local_lat < rows_dev) & (local_lon >= 0) & (local_lon < cols_dev)
        )
        picked = layered_arrays[0][
            :, jnp.clip(local_lat, 0, rows_dev - 1), jnp.clip(local_lon, 0, cols_dev - 1)
        ]
        owned, share = (owned, jnp.where(owned[:, None], jnp.transpose(picked), 0.0))
        link_share = jnp.where(owned[:, None], weights[None, :], 0.0)
        priors, links = lax.psum((share, link_share), ("lon", "lat"))
        current = priors
        values = obs_value[batch]
        variances = obs_variance[batch]

        def turn(k, carry):
            current, transform = carry
            delta, slope = increments(current[0 + k], values[k], variances[k], ensemble_snapshots)
            coef = links[:, k] * jnp.dot(current, slope, precision=lax.Precision.HIGHEST)
            current = current + coef[:, None] * delta[None, :]
            lifted = jnp.dot(transform, slope, precision=lax.Precision.HIGHEST)
            transform = transform + weights[k] * lifted[:, None] * delta[None, :]
            return (current, transform)

        start = (current, jnp.eye(ensemble_snapshots, dtype=jnp.float32))
        priors, transform = lax.fori_loop(0, values.shape[0], turn, start)
        flat = layered_arrays.reshape(3, ensemble_snapshots, rows_dev * cols_dev)
        flat = jnp.einsum("fmc,mn->fnc", flat, transform, precision=lax.Precision.HIGHEST)
        layered_arrays = flat.reshape(3, ensemble_snapshots, rows_dev, cols_dev)
    return layered_arrays


def solution(mesh):
    in_specs = (P(None, None, "lat", "lon"), P(), P(), P(), P(None, None, ("lon", "lat")))
    out_specs = P(None, None, "lat", "lon")
    return jax.shard_map(body, mesh=mesh, in_specs=in_specs, out_specs=out_specs, check_vma=False)
```

profile of v0, /device:TPU:1, one launch (start us, length us, event | category | flops | bytes accessed | tf_op | source)
XLA Modules:
  0.0 1564.8 jit_solution(3052727789203817203)
XLA Ops:
  1.7 4.0 collective-permute-start
  5.9 14.0 collective-permute-start.1
  20.7 16.9 %collective-permute-start.2 = (f32[2,64,1,130]{1,3,2,0:T(8,128)S(1)}, f32[2,64,1,130]{1,3,2,0:T(8,128)S(1)}, u32[]{:S(2)}, u32[]{:S(2)}) collective-permute-start(f32[2,64,1,130]{1,3,2,0:T(8,128)S(1)} %get-tuple-element.439), channel_id=1, source_target_pairs={{0,1},{1,2},{2,3},{3,4},{4,5},{5,6},{6,7},{7,8},{8,9},{9,10},{10,1... | collective-permute-start | bytes 199688 | tf_op jit(solution)/shard_map/ppermute | solution.py:23
  39.5 2.4 collective-permute-done.2
  41.9 15.3 collective-permute-done.3
  59.5 13.6 collective-permute-start.5
  73.9 2.6 collective-permute-start.6
  78.9 12.0 collective-permute-done.7
  93.2 12.6 collective-permute-start.9
  106.6 2.7 collective-permute-start.10
  111.3 13.8 collective-permute-done.11
  127.5 13.0 collective-permute-start.13
  141.2 2.6 collective-permute-start.14
  146.2 12.2 collective-permute-done.15
  160.8 12.6 collective-permute-start.17
  173.5 5.5 collective-permute-done.16
  181.0 8.2 collective-permute-start.19
  189.2 6.9 collective-permute-done.19
  199.2 12.1 collective-permute-start.21
  212.0 2.9 collective-permute-start.22
  214.9 11.7 collective-permute-start.23
  226.7 2.7 collective-permute-done.23
  231.7 15.6 %collective-permute-start.25 = (f32[2,64,8,1]{1,3,2,0:T(1,128)S(1)}, f32[2,64,8,1]{1,3,2,0:T(1,128)S(1)}, u32[]{:S(2)}, u32[]{:S(2)}) collective-permute-start(f32[2,64,8,1]{1,3,2,0:T(1,128)S(1)} %get-tuple-element.442), channel_id=1, source_target_pairs={{32,0},{64,32},{96,64},{128,96},{160,128},{192,160},{224,192},{256... | collective-permute-start | bytes 12296 | tf_op jit(solution)/shard_map/ppermute | solution.py:25
  248.2 2.5 collective-permute-start.26
  250.8 11.4 collective-permute-start.27
  262.2 3.7 collective-permute-done.27
  271.0 12.6 collective-permute-start.29
  283.8 166.1 %all-reduce.1 = (f32[64,64]{1,0:T(8,128)S(1)}, f32[64,64]{1,0:T(8,128)S(1)}) all-reduce(f32[64,64]{1,0:T(8,128)S(1)} %get-tuple-element.482, f32[64,64]{1,0:T(8,128)S(1)} %get-tuple-element.481), channel_id=1, replica_groups=mesh['lon'=32,'lat'=32] {'lon','lat'}, use_global_device_ids=true, to_apply=%region_0.1 | all-reduce | flops 8192 | bytes 65536 | tf_op jit(solution)/shard_map/psum | solution.py:109
  450.0 5.6 collective-permute-start.30
  457.6 458.9 %while.34 = (s32[]{:T(128)}, f32[64,64]{1,0:T(8,128)S(1)}, f32[64,64]{1,0:T(8,128)S(1)}, f32[64,64]{0,1:T(8,128)S(1)}, f32[64]{0:T(128)S(1)}, /*index=5*/f32[64]...) while((s32[]{:T(128)}, f32[64,64]{1,0:T(8,128)S(1)}, ...), condition=%wide.region_5.6_spmd, body=%wide.region_2.5_spmd.sunk | while | flops 115344 | bytes 102053 | solution.py:124
  919.5 160.4 %all-reduce = (f32[64,64]{1,0:T(8,128)S(1)}, f32[64,64]{1,0:T(8,128)S(1)}) all-reduce(f32[64,64]{1,0:T(8,128)S(1)} %get-tuple-element.480, f32[64,64]{1,0:T(8,128)S(1)} %get-tuple-element.479), channel_id=1, replica_groups=mesh['lon'=32,'lat'=32] {'lon','lat'}, use_global_device_ids=true, to_apply=%region_6.7 | all-reduce | flops 8192 | bytes 65536 | tf_op jit(solution)/shard_map/psum | solution.py:109
  1080.0 483.0 %while.35 = (s32[]{:T(128)}, f32[64,64]{1,0:T(8,128)S(1)}, f32[64,64]{1,0:T(8,128)S(1)}, f32[64,64]{0,1:T(8,128)S(1)}, f32[64]{0:T(128)S(1)}, /*index=5*/f32[64]...) while((s32[]{:T(128)}, f32[64,64]{1,0:T(8,128)S(1)}, ...), condition=%wide.region_11.12_spmd, body=%wide.region_8.11_spmd.sunk | while | flops 115344 | bytes 102053 | solution.py:124
  (1270 shorter events, 556.0 us)
Async XLA Ops:
  1.7 18.9 %collective-permute-start = (f32[2,64,8,1]{1,3,2,0:T(1,128)S(1)}, f32[2,64,8,1]{1,3,2,0:T(1,128)S(1)}, u32[]{:S(2)}, u32[]{:S(2)}) collective-permute-start(f32[2,64,8,1]{1,3,2,0:T(1,128)S(1)} %copy.29), channel_id=1, source_target_pairs={{0,32},{32,64},{64,96},{96,128},{128,160},{160,192},{192,224},{224... | collective-permute-start | bytes 12296 | tf_op jit(solution)/shard_map/ppermute | solution.py:23
  5.9 14.8 collective-permute-start.1
  20.7 21.2 %collective-permute-start.2 = (f32[2,64,1,130]{1,3,2,0:T(8,128)S(1)}, f32[2,64,1,130]{1,3,2,0:T(8,128)S(1)}, u32[]{:S(2)}, u32[]{:S(2)}) collective-permute-start(f32[2,64,1,130]{1,3,2,0:T(8,128)S(1)} %get-tuple-element.439), channel_id=1, source_target_pairs={{0,1},{1,2},{2,3},{3,4},{4,5},{5,6},{6,7},{7,8},{8,9},{9,10},{10,1... | collective-permute-start | bytes 199688 | tf_op jit(solution)/shard_map/ppermute | solution.py:23
  37.6 19.6 %collective-permute-start.3 = (f32[2,64,1,130]{1,3,2,0:T(8,128)S(1)}, f32[2,64,1,130]{1,3,2,0:T(8,128)S(1)}, u32[]{:S(2)}, u32[]{:S(2)}) collective-permute-start(f32[2,64,1,130]{1,3,2,0:T(8,128)S(1)} %get-tuple-element.440), channel_id=1, source_target_pairs={{1,0},{2,1},{3,2},{4,3},{5,4},{6,5},{7,6},{8,7},{9,8},{10,9},{11,1... | collective-permute-start | bytes 199688 | tf_op jit(solution)/shard_map/ppermute | solution.py:25
  57.6 15.5 collective-permute-start.4
  59.5 14.3 collective-permute-start.5
  73.9 5.0 collective-permute-start.6
  76.5 14.4 collective-permute-start.7
  91.3 14.5 collective-permute-start.8
  93.2 13.3 collective-permute-start.9
  106.6 4.7 collective-permute-start.10
  109.3 15.8 %collective-permute-start.11 = (f32[2,64,1,130]{1,3,2,0:T(8,128)S(1)}, f32[2,64,1,130]{1,3,2,0:T(8,128)S(1)}, u32[]{:S(2)}, u32[]{:S(2)}) collective-permute-start(f32[2,64,1,130]{1,3,2,0:T(8,128)S(1)} %get-tuple-element.438), channel_id=1, source_target_pairs={{1,0},{2,1},{3,2},{4,3},{5,4},{6,5},{7,6},{8,7},{9,8},{10,9},{11,1... | collective-permute-start | bytes 199688 | tf_op jit(solution)/shard_map/ppermute | solution.py:25
  125.5 14.9 collective-permute-start.12
  127.5 13.7 collective-permute-start.13
  141.2 5.0 collective-permute-start.14
  143.9 14.5 collective-permute-start.15
  158.9 20.1 %collective-permute-start.16 = (f32[2,64,8,1]{1,3,2,0:T(1,128)S(1)}, f32[2,64,8,1]{1,3,2,0:T(1,128)S(1)}, u32[]{:S(2)}, u32[]{:S(2)}) collective-permute-start(f32[2,64,8,1]{1,3,2,0:T(1,128)S(1)} %get-tuple-element.443), channel_id=1, source_target_pairs={{0,32},{32,64},{64,96},{96,128},{128,160},{160,192},{192,224},{224... | collective-permute-start | bytes 12296 | tf_op jit(solution)/shard_map/ppermute | solution.py:23
  160.8 18.2 %collective-permute-start.17 = (f32[2,64,8,1]{1,3,2,0:T(1,128)S(1)}, f32[2,64,8,1]{1,3,2,0:T(1,128)S(1)}, u32[]{:S(2)}, u32[]{:S(2)}) collective-permute-start(f32[2,64,8,1]{1,3,2,0:T(1,128)S(1)} %get-tuple-element.444), channel_id=1, source_target_pairs={{32,0},{64,32},{96,64},{128,96},{160,128},{192,160},{224,192},{256... | collective-permute-start | bytes 12296 | tf_op jit(solution)/shard_map/ppermute | solution.py:25
  179.0 10.1 collective-permute-start.18
  181.0 15.1 collective-permute-start.19
  197.2 14.0 collective-permute-start.20
  199.2 12.8 collective-permute-start.21
  212.0 14.6 collective-permute-start.22
  214.9 14.4 collective-permute-start.23
  229.8 17.6 %collective-permute-start.24 = (f32[2,64,8,1]{1,3,2,0:T(1,128)S(1)}, f32[2,64,8,1]{1,3,2,0:T(1,128)S(1)}, u32[]{:S(2)}, u32[]{:S(2)}) collective-permute-start(f32[2,64,8,1]{1,3,2,0:T(1,128)S(1)} %get-tuple-element.441), channel_id=1, source_target_pairs={{0,32},{32,64},{64,96},{96,128},{128,160},{160,192},{192,224},{224... | collective-permute-start | bytes 12296 | tf_op jit(solution)/shard_map/ppermute | solution.py:23
  231.7 16.4 %collective-permute-start.25 = (f32[2,64,8,1]{1,3,2,0:T(1,128)S(1)}, f32[2,64,8,1]{1,3,2,0:T(1,128)S(1)}, u32[]{:S(2)}, u32[]{:S(2)}) collective-permute-start(f32[2,64,8,1]{1,3,2,0:T(1,128)S(1)} %get-tuple-element.442), channel_id=1, source_target_pairs={{32,0},{64,32},{96,64},{128,96},{160,128},{192,160},{224,192},{256... | collective-permute-start | bytes 12296 | tf_op jit(solution)/shard_map/ppermute | solution.py:25
  248.2 14.0 collective-permute-start.26
  250.8 15.1 collective-permute-start.27
  269.1 180.8 %collective-permute-start.28 = (f32[64,8,1]{0,2,1:T(1,128)S(1)}, f32[64,8,1]{0,2,1:T(1,128)S(1)}, u32[]{:S(2)}, u32[]{:S(2)}) collective-permute-start(f32[64,8,1]{0,2,1:T(1,128)S(1)} %get-tuple-element.460), channel_id=1, source_target_pairs={{0,32},{32,64},{64,96},{96,128},{128,160},{160,192},{192,224},{224... | collective-permute-start | bytes 6152 | tf_op jit(solution)/shard_map/ppermute | solution.py:23
  271.0 178.9 %collective-permute-start.29 = (f32[64,8,1]{0,2,1:T(1,128)S(1)}, f32[64,8,1]{0,2,1:T(1,128)S(1)}, u32[]{:S(2)}, u32[]{:S(2)}) collective-permute-start(f32[64,8,1]{0,2,1:T(1,128)S(1)} %get-tuple-element.461), channel_id=1, source_target_pairs={{32,0},{64,32},{96,64},{128,96},{160,128},{192,160},{224,192},{256... | collective-permute-start | bytes 6152 | tf_op jit(solution)/shard_map/ppermute | solution.py:25
  450.0 466.7 %collective-permute-start.30 = (f32[64,1,130]{0,2,1:T(8,128)S(1)}, f32[64,1,130]{0,2,1:T(8,128)S(1)}, u32[]{:S(2)}, u32[]{:S(2)}) collective-permute-start(f32[64,1,130]{0,2,1:T(8,128)S(1)} %get-tuple-element.452), channel_id=1, source_target_pairs={{0,1},{1,2},{2,3},{3,4},{4,5},{5,6},{6,7},{7,8},{8,9},{9,10},{10,1... | collective-permute-start | bytes 99848 | tf_op jit(solution)/shard_map/ppermute | solution.py:23
  455.6 461.1 %collective-permute-start.31 = (f32[64,1,130]{0,2,1:T(8,128)S(1)}, f32[64,1,130]{0,2,1:T(8,128)S(1)}, u32[]{:S(2)}, u32[]{:S(2)}) collective-permute-start(f32[64,1,130]{0,2,1:T(8,128)S(1)} %get-tuple-element.453), channel_id=1, source_target_pairs={{1,0},{2,1},{3,2},{4,3},{5,4},{6,5},{7,6},{8,7},{9,8},{10,9},{11,1... | collective-permute-start | bytes 99848 | tf_op jit(solution)/shard_map/ppermute | solution.py:25
  (10 other events, 1128.6 us)
where the time goes:
time: 1580 us; the launch traced here: 1560 us
  loops' own time  430 us (27%)
  blocking collectives  327 us (21%)
  local copies, waits for them, and re-layouts  236 us (15%)
  starting transfers between devices  203 us (13%)
  other arithmetic  176 us (11%)
  matrix products  116 us (7%)
  waiting for transfers between devices  78.2 us (5%)
    another operation x2, loops' own time, body(): priors, transform = lax.fori_loop(0, values.shape[0], turn, start)  430 us
    psum x2, blocking collectives, body(): priors, links = lax.psum((share, link_share), ('lon', 'lat'))  327 us
    ppermute x16, starting transfers between devices, with_halo(): lax.ppermute(head, axis, [((i + 1) % count, i) for i in range(count)])  147 us
    dot_general x128, matrix products, turn(): lifted = jnp.dot(transform, slope, precision=lax.Precision.HIGHEST)  95.4 us
    dynamic_slice x128, local copies, waits for them, and re-layouts, turn(): values[k]  78.4 us
    dynamic_slice x128, local copies, waits for them, and re-layouts, turn(): transform = transform + weights[k] * lifted[:, None] * delta[None, :]  76.7 us
    reduce_sum x128, other arithmetic, increments(): jnp.sum(spread_dev * spread_dev) / (ensemble_snapshots - 1) + SMALL_EPSILON  76.5 us
    reduce_sum x128, other arithmetic, increments(): center = jnp.mean(prior)  76 us
  transfers between devices with their start and end apart: 32, of which 16 were waited for; matrix products, arithmetic and copies ran while one was open for 16% of the time, Pallas kernels for 0%

commit v1 on v0

v1 whole, which is shorter than its diff:
```python
import functools

import jax
import jax.numpy as jnp
from jax import lax
from jax.experimental import pallas as pl
from jax.experimental.pallas import tpu as pltpu
from jax.sharding import PartitionSpec as P

MESH = pl.DeviceIdType.MESH
F32 = jnp.float32
BF16 = jnp.bfloat16

STEPS = 4
LOC_RADIUS = 256
CORIOLIS = 0.1
SMALL_EPSILON = 1e-06
MEMBERS = 64
ROWS = 8
COLS = 128
GROUPS = 8
HALVES = 2 * STEPS
EXT = HALVES - 1
PICK_ROWS = ROWS + 2 * EXT


class Geometry:
    def __init__(self, n_lon, n_lat):
        self.n_lon, self.n_lat = n_lon, n_lat
        if (n_lon, n_lat) == (32, 32):
            self.x, self.y, self.zh, self.c = 4, 4, 4, 2
        else:
            self.x, self.y, self.zh, self.c = 1, 1, n_lat // 2, 2
        self.zl = n_lon // self.x
        self.near = self.x * self.y * self.c
        self.far = self.zl * self.zh
        self.total_rows = ROWS * n_lat
        self.total_cols = COLS * n_lon

    def near_index(self, lon, lat):
        return (lon % self.x) * (self.y * self.c) + (lat // (self.zh * self.c)) * self.c + lat % self.c

    def near_peer(self, i, lon, lat):
        x, y, c = i // (self.y * self.c), (i // self.c) % self.y, i % self.c
        return (lon // self.x) * self.x + x, (y * self.zh + (lat // self.c) % self.zh) * self.c + c

    def far_index(self, lon, lat):
        return ((lat // self.c) % self.zh) * self.zl + lon // self.x

    def far_peer(self, i, lon, lat):
        zh, zl = i // self.zl, i % self.zl
        return zl * self.x + lon % self.x, ((lat // (self.zh * self.c)) * self.zh + zh) * self.c + lat % self.c


def iota(shape, dim):
    return lax.broadcasted_iota(jnp.int32, shape, dim)


def roll(v, shift):
    return pltpu.roll(v, shift % COLS, 1)


def pack_edges(tiles):
    lane = iota((8, COLS), 1)
    out = None
    for s, t in enumerate(tiles):
        r = roll(t, 16 * s + 8)
        out = r if out is None else jnp.where(lane // 16 == s, r, out)
    return out


def unpack_edges(packed, s):
    return roll(packed, -(16 * s + 8))


def lon_diff(m, s, first, last):
    mp, sp, mm, sm = roll(m, -1), roll(s, -1), roll(m, 1), roll(s, 1)
    return (
        jnp.where(last, sp, mp) - jnp.where(first, sm, mm),
        jnp.where(last, mp, sp) - jnp.where(first, mm, sm),
    )


def column_of(row, eye):
    return jnp.sum(jnp.where(eye, row, 0.0), axis=1, keepdims=True)


class Sum:
    def __init__(self, geo, lon, lat, refs, sems):
        self.geo, self.lon, self.lat = geo, lon, lat
        self.src, self.near, self.mid, self.far, self.last, self.out = refs
        self.sems = sems
        self.me = geo.near_index(lon, lat)
        self.me_far = geo.far_index(lon, lat)

    def _send(self, stage, src, dst, n, me, peer):
        def one(i, carry):
            p = lax.rem(me + i, n)
            pltpu.make_async_remote_copy(
                src_ref=src(p),
                dst_ref=dst.at[me],
                send_sem=self.sems.at[0, stage],
                recv_sem=self.sems.at[1, stage],
                device_id=peer(p, self.lon, self.lat),
                device_id_type=MESH,
            ).start()
            return carry

        lax.fori_loop(1, n, one, 0)

    def _wait(self, stage, buf, n):
        if n > 1:
            part = buf.at[pl.ds(0, n - 1)]
            pltpu.make_async_copy(part, part, self.sems.at[1, stage]).wait()

    def _added(self, buf, n):
        total = buf[0]
        for i in range(1, n):
            total = total + buf[i]
        return total

    def send_near(self):
        self.near[self.me] = self.src[self.me]
        self._send(0, lambda p: self.src.at[p], self.near, self.geo.near, self.me, self.geo.near_peer)

    def send_far(self):
        self._wait(0, self.near, self.geo.near)
        total = self._added(self.near, self.geo.near)
        self.mid[...] = total
        self.far[self.me_far] = total
        self._send(1, lambda p: self.mid, self.far, self.geo.far, self.me_far, self.geo.far_peer)

    def send_last(self):
        self._wait(1, self.far, self.geo.far)
        total = self._added(self.far, self.geo.far)
        self.last[...] = total
        self.out[self.me] = total
        self._send(2, lambda p: self.last, self.out, self.geo.near, self.me, self.geo.near_peer)

    def wait_last(self):
        self._wait(2, self.out, self.geo.near)

    def wait_sends(self):
        for stage, buf, n in ((0, self.near, self.geo.near), (1, self.far, self.geo.far), (2, self.out, self.geo.near)):
            if n > 1:
                part = buf.at[pl.ds(0, n - 1)]
                pltpu.make_async_copy(part, part, self.sems.at[0, stage]).wait()


def forecast_kernel(
    geo, x_ref, cell_ref, value_ref, variance_ref, mask_ref,
    f_ref, c_ref, y_ref,
    main, side, edges, edges_in, series, series_in, ghosts, heights, onehot,
    l0, l1, l2, l3, l4, l5, p0, p1, p2, p3, p4, p5,
    lon_sems, lat_sems, l_sems, p_sems,
):
    lon, lat = lax.axis_index("lon"), lax.axis_index("lat")
    n_lon, n_lat = geo.n_lon, geo.n_lat
    east, west = lax.rem(lon + 1, n_lon), lax.rem(lon + n_lon - 1, n_lon)
    after, before = lax.rem(lat + 1, n_lat), lax.rem(lat + n_lat - 1, n_lat)
    links = Sum(geo, lon, lat, (l0, l1, l2, l3, l4, l5), l_sems)
    priors = Sum(geo, lon, lat, (p0, p1, p2, p3, p4, p5), p_sems)

    barrier = pltpu.get_barrier_semaphore()
    for d in ((east, lat), (west, lat), (lon, after), (lon, before)):
        pl.semaphore_signal(barrier, inc=1, device_id=d, device_id_type=MESH)

    def greet(n, me, peer):
        def one(i, carry):
            pl.semaphore_signal(barrier, inc=1, device_id=peer(lax.rem(me + i, n), lon, lat), device_id_type=MESH)
            return carry

        lax.fori_loop(1, n, one, 0)

    greet(geo.far, links.me_far, geo.far_peer)
    greet(geo.near, links.me, geo.near_peer)

    row_first, col_first = lat * ROWS, lon * COLS

    def field_row(f, g, r):
        return x_ref[f, pl.ds(g * 64 + r, 8, stride=8), :]

    def pack(g, carry):
        for f in range(3):
            edges[g, f] = pack_edges([field_row(f, g, r) for r in range(ROWS)])
        return carry

    lax.fori_loop(0, GROUPS, pack, 0)

    lane = iota((8, COLS), 1)
    first, last = lane == 0, lane == COLS - 1
    big_row, big_col = iota((128, 128), 0), iota((128, 128), 1)
    eye = big_row == big_col
    cells = jnp.concatenate([cell_ref[0:1, :], cell_ref[1:2, :]], axis=1)
    obs_row, obs_col = cells // geo.total_cols, cells % geo.total_cols
    match_col = big_row + col_first == obs_col
    for i in range(PICK_ROWS):
        hit = match_col & (obs_row == row_first + (i - EXT))
        onehot[i * 128:(i + 1) * 128, :] = jnp.where(hit, 1.0, 0.0).astype(BF16)
    owned = jnp.where((obs_row // ROWS == lat) & (obs_col // COLS == lon), 1.0, 0.0)
    mask_col = mask_ref[...].astype(F32)
    share = mask_col * owned
    per = 128 // geo.near
    for i in range(geo.near):
        l0[i] = share[i * per:(i + 1) * per, :]
    cells_col = column_of(cells.astype(F32), eye).astype(jnp.int32)
    row_col, col_col = cells_col // geo.total_cols, cells_col % geo.total_cols

    def damping(centre_row, centre_col):
        row_gap = row_col - centre_row
        col_gap = jnp.abs(col_col - centre_col)
        col_gap = jnp.minimum(col_gap, geo.total_cols - col_gap)
        distance = (row_gap * row_gap + col_gap * col_gap).astype(F32)
        return 1.0 + distance / (LOC_RADIUS * LOC_RADIUS)

    own = mask_col / damping(row_first + ROWS // 2, col_first + COLS // 2)
    value_col = column_of(jnp.concatenate([value_ref[0:1, :], value_ref[1:2, :]], axis=1), eye)
    variance_col = column_of(jnp.concatenate([variance_ref[0:1, :], variance_ref[1:2, :]], axis=1), eye)
    c_ref[1] = jnp.broadcast_to(1.0 / variance_col, (128, 128))
    c_ref[2] = jnp.broadcast_to(value_col, (128, 128))
    c_ref[3] = jnp.broadcast_to(own, (128, 128))

    pl.semaphore_wait(barrier, 4 + (geo.far - 1) + (geo.near - 1))

    def lon_copies(g):
        return [
            pltpu.make_async_remote_copy(
                src_ref=edges.at[g], dst_ref=edges_in.at[s, g], send_sem=lon_sems.at[0, s, g], recv_sem=lon_sems.at[1, s, g],
                device_id=(d, lat), device_id_type=MESH,
            )
            for s, d in ((0, east), (1, west))
        ]

    def lat_copies(g):
        return [
            pltpu.make_async_remote_copy(
                src_ref=series.at[s, g], dst_ref=series_in.at[1 - s, g], send_sem=lat_sems.at[0, s, g],
                recv_sem=lat_sems.at[1, 1 - s, g], device_id=(lon, d), device_id_type=MESH,
            )
            for s, d in ((0, before), (1, after))
        ]

    def start_lon(g, carry):
        for c in lon_copies(g):
            c.start()
        return carry

    lax.fori_loop(0, GROUPS, start_lon, 0)
    links.send_near()

    has_before = jnp.where(lat > 0, 1.0, 0.0)
    has_after = jnp.where(lat < n_lat - 1, 1.0, 0.0)

    def turning(r):
        row = (row_first + r).astype(F32)
        return CORIOLIS * ((2.0 * row + 1.0) / geo.total_rows - 1.0)

    def fit(r, v):
        return v * has_before if r < 0 else v * has_after if r >= ROWS else v

    class State:
        def __init__(self, g):
            self.rows = [set(range(ROWS)) for _ in range(3)]
            from_west = lane % 16 < 8
            for f in range(3):
                packed = jnp.where(from_west, edges_in[0, g, f], edges_in[1, g, f])
                for r in range(ROWS):
                    main[f, r + 8] = field_row(f, g, r)
                    side[f, r + 8] = unpack_edges(packed, r)

        def get(self, f, r):
            if r not in self.rows[f]:
                return None
            return main[f, r + 8], side[f, r + 8]

        def put(self, f, r, v):
            self.rows[f].add(r)
            main[f, r + 8], side[f, r + 8] = v

    def less(a, b):
        if a is None and b is None:
            return None
        if b is None:
            return a
        if a is None:
            return tuple(-q for q in b)
        return tuple(p - q for p, q in zip(a, b))

    def plus(a, b):
        if a is None or b is None:
            return a if b is None else b
        return tuple(p + q for p, q in zip(a, b))

    def scaled(a, k):
        return None if a is None else tuple(p * k for p in a)

    def lon_of(v):
        return None if v is None else lon_diff(v[0], v[1], first, last)

    def half_step(st, p, lo, hi, ghost=None):
        at = (lambda f, r: ghost[r] if ghost is not None and r in ghost else st.get(f, r))
        for r in range(lo, hi):
            if p % 2:
                slope = plus(lon_of(st.get(1, r)), less(at(2, r + 1), at(2, r - 1)))
                new = less(st.get(0, r), scaled(slope, 0.25))
                st.put(0, r, tuple(fit(r, v) for v in new))
            else:
                e, n, k = st.get(1, r), st.get(2, r), turning(r)
                new_e = less(plus(e, scaled(n, k)), scaled(lon_of(st.get(0, r)), 0.25))
                new_n = less(less(n, scaled(e, k)), scaled(less(at(0, r + 1), at(0, r - 1)), 0.25))
                if new_e is not None:
                    st.put(1, r, tuple(fit(r, v) for v in new_e))
                if new_n is not None:
                    st.put(2, r, tuple(fit(r, v) for v in new_n))

    def spread(g, carry):
        for c in lon_copies(g):
            c.wait_recv()
        st = State(g)
        sides = ([], [])
        for p in range(HALVES):
            if p > 0:
                half_step(st, p, -p, ROWS + p)
            f = 0 if p % 2 else 2
            for s, (r, outside) in enumerate(((0, -1), (ROWS - 1, ROWS))):
                m, e = st.get(f, r)
                series[s, g, p] = m
                sides[s].append(e)
                if p > 0:
                    ghosts[g, s, p, 0], ghosts[g, s, p, 1] = st.get(f, outside)
        for s in range(2):
            series[s, g, HALVES] = pack_edges(sides[s])
        for c in lat_copies(g):
            c.start()
        for i in range(PICK_ROWS):
            heights[pl.ds(pl.multiple_of(g * 8, 8), 8), i * 128:(i + 1) * 128] = main[0, i - EXT + 8]
        return carry

    lax.fori_loop(0, GROUPS, spread, 0)

    total = jnp.zeros((3 * MEMBERS, 128), F32)
    for i in range(PICK_ROWS // 2):
        v = heights[:, i * 256:(i + 1) * 256]
        high = v.astype(BF16)
        rest = v - high.astype(F32)
        middle = rest.astype(BF16)
        low = (rest - middle.astype(F32)).astype(BF16)
        total = total + jnp.dot(
            jnp.concatenate([high, middle, low], axis=0), onehot[i * 256:(i + 1) * 256, :], preferred_element_type=F32
        )
    picked = total[:MEMBERS] + (total[MEMBERS:2 * MEMBERS] + total[2 * MEMBERS:])
    few = MEMBERS // geo.near
    for i in range(geo.near):
        p0[i] = picked[i * few:(i + 1) * few, :]
    priors.send_near()
    links.send_far()
    priors.send_far()

    def settle(g, carry):
        for c in lat_copies(g):
            c.wait_recv()
        st = State(g)
        packed = [series_in[s, g, HALVES] for s in range(2)]
        for p in range(1, HALVES + 1):
            ghost = {}
            for s, (outside, there) in enumerate(((-1, has_before), (ROWS, has_after))):
                v = (series_in[s, g, p - 1] * there, unpack_edges(packed[s], p - 1) * there)
                if p > 1:
                    v = plus(v, (ghosts[g, s, p - 1, 0], ghosts[g, s, p - 1, 1]))
                ghost[outside] = v
            half_step(st, p, 0, ROWS, ghost)
        for f in range(3):
            for r in range(ROWS):
                f_ref[f * ROWS + r, pl.ds(pl.multiple_of(g * 8, 8), 8), :] = main[f, r + 8]
        return carry

    lax.fori_loop(0, 2, settle, 0)
    links.send_last()
    priors.send_last()
    links.wait_last()
    for i in range(geo.near):
        c_ref[0, i * per:(i + 1) * per, :] = l5[i]
    weighted = c_ref[0] / damping(obs_row // ROWS * ROWS + ROWS // 2, obs_col // COLS * COLS + COLS // 2)
    c_ref[0] = weighted
    beside = jnp.sum(jnp.where(big_col == big_row + 1, weighted, 0.0), axis=1, keepdims=True)
    c_ref[4] = jnp.broadcast_to(beside, (128, 128))
    lax.fori_loop(2, GROUPS, settle, 0)
    priors.wait_last()
    for i in range(geo.near):
        y_ref[i * few:(i + 1) * few, :] = p5[i]

    links.wait_sends()
    priors.wait_sends()

    def finish(g, carry):
        for c in lon_copies(g) + lat_copies(g):
            c.wait_send()
        return carry

    lax.fori_loop(0, GROUPS, finish, 0)


def added_sublanes(v):
    t = v.reshape(8, 8, COLS).sum(axis=0)
    for s in (4, 2, 1):
        t = t + pltpu.roll(t, s, 0)
    return t


def tall(v):
    return jnp.concatenate([v] * 8, axis=0)


def across(column):
    return jnp.broadcast_to(column, (column.shape[0], COLS))


def update_kernel(n_obs, f_ref, c_ref, y_ref, out_ref):
    y = y_ref[...]
    mean = added_sublanes(y) * (1.0 / MEMBERS)
    b = y - tall(mean)
    a = jnp.where(iota((MEMBERS, COLS), 0) == iota((MEMBERS, COLS), 1), 1.0, 0.0)
    a_mean = jnp.zeros((8, COLS), F32)
    left = iota((8, COLS), 1) < MEMBERS

    def row(i, k):
        return jnp.broadcast_to(c_ref[i, k:k + 1, :], (8, COLS))

    d, m = across(b[:, 0:1]), across(mean[:, 0:1])
    for k in range(2 * n_obs):
        if k == n_obs:
            a, a_mean = jnp.where(tall(left), a, b), jnp.where(left, a_mean, mean)
        later = k >= n_obs
        obs, obs_mean = (a, a_mean) if later else (b, mean)
        if k + 1 < 2 * n_obs:
            d_next, m_next = across(obs[:, k + 1:k + 2]), across(obs_mean[:, k + 1:k + 2])
        s = added_sublanes(d * d) * (1.0 / (MEMBERS - 1)) + SMALL_EPSILON
        ratio = s * row(1, k)
        root = lax.rsqrt(1.0 + ratio)
        gain = root - 1.0
        shift = ratio * (root * root) * (row(2, k) - m)
        scale = 1.0 / ((MEMBERS - 1) * s)
        if k + 1 < 2 * n_obs:
            c = row(4, k) * scale * added_sublanes(d_next * d)
            new_d, new_m = d_next + tall(c * gain) * d, m_next + c * shift
        link, own = row(0, k), row(3, k)
        c = (jnp.where(left, own, link) if later else own) * scale * added_sublanes(a * d)
        a, a_mean = a + tall(c * gain) * d, a_mean + c * shift
        if not later:
            c = link * scale * added_sublanes(b * d)
            b, mean = b + tall(c * gain) * d, mean + c * shift
        if k + 1 < 2 * n_obs:
            d, m = new_d, new_m
    t = (a + tall(a_mean))[:, :MEMBERS]
    t_high = t.astype(BF16)
    t_low = (t - t_high.astype(F32)).astype(BF16)
    lhs = jnp.concatenate([t_high, t_high, t_low, t_low], axis=1)
    for i in range(0, 3 * ROWS, 2):
        v = jnp.concatenate([f_ref[i], f_ref[i + 1]], axis=1)
        high = v.astype(BF16)
        low = (v - high.astype(F32)).astype(BF16)
        r = jnp.dot(lhs, jnp.concatenate([high, low, high, low], axis=0), preferred_element_type=F32)
        for q in range(2):
            out_ref[(i + q) // ROWS, pl.ds((i + q) % ROWS, MEMBERS, stride=ROWS), :] = r[:, q * COLS:(q + 1) * COLS]


def body(geo, model_variables, obs_cell, obs_value, obs_variance, tile_mask):
    vmem = pl.BlockSpec(memory_space=pltpu.VMEM)
    x = model_variables.reshape(3, MEMBERS * ROWS, COLS)
    mask = tile_mask.reshape(128, 1)
    n, few, per = geo.near, MEMBERS // geo.near, 128 // geo.near

    def sum_buffers(rows):
        v = functools.partial(pltpu.VMEM, dtype=F32)
        return [
            v((n, rows, 128)), v((n, rows, 128)), v((rows, 128)), v((geo.far, rows, 128)), v((rows, 128)), v((n, rows, 128)),
        ]

    dma = pltpu.SemaphoreType.DMA
    f, c, y = pl.pallas_call(
        functools.partial(forecast_kernel, geo),
        out_shape=(
            jax.ShapeDtypeStruct((3 * ROWS, MEMBERS, COLS), F32),
            jax.ShapeDtypeStruct((5, 128, 128), F32),
            jax.ShapeDtypeStruct((MEMBERS, 128), F32),
        ),
        in_specs=[vmem] * 5,
        out_specs=(vmem, vmem, vmem),
        scratch_shapes=[
            pltpu.VMEM((3, 24, 8, COLS), F32),
            pltpu.VMEM((3, 24, 8, COLS), F32),
            pltpu.VMEM((GROUPS, 3, 8, COLS), F32),
            pltpu.VMEM((2, GROUPS, 3, 8, COLS), F32),
            pltpu.VMEM((2, GROUPS, HALVES + 1, 8, COLS), F32),
            pltpu.VMEM((2, GROUPS, HALVES + 1, 8, COLS), F32),
            pltpu.VMEM((GROUPS, 2, HALVES, 2, 8, COLS), F32),
            pltpu.VMEM((MEMBERS, PICK_ROWS * COLS), F32),
            pltpu.VMEM((PICK_ROWS * COLS, 128), BF16),
            *sum_buffers(per),
            *sum_buffers(few),
            dma((2, 2, GROUPS)), dma((2, 2, GROUPS)), dma((2, 3)), dma((2, 3)),
        ],
        compiler_params=pltpu.CompilerParams(collective_id=0, has_side_effects=True, vmem_limit_bytes=40 * 2**20),
    )(x, obs_cell, obs_value, obs_variance, mask)
    out = pl.pallas_call(
        functools.partial(update_kernel, obs_cell.shape[1]),
        out_shape=jax.ShapeDtypeStruct((3, MEMBERS * ROWS, COLS), F32),
        in_specs=[vmem] * 3,
        out_specs=vmem,
        compiler_params=pltpu.CompilerParams(vmem_limit_bytes=32 * 2**20),
    )(f, c, y)
    return out.reshape(3, MEMBERS, ROWS, COLS)


def solution(mesh):
    geo = Geometry(mesh.shape["lon"], mesh.shape["lat"])
    in_specs = (P(None, None, "lat", "lon"), P(), P(), P(), P(None, None, ("lon", "lat")))
    out_specs = P(None, None, "lat", "lon")
    return jax.shard_map(
        functools.partial(body, geo), mesh=mesh, in_specs=in_specs, out_specs=out_specs, check_vma=False
    )
```

time: 1580 us -> 99 us (0.06)
  loops' own time: 430 us -> 0 us
  blocking collectives: 327 us -> 0 us
  local copies, waits for them, and re-layouts: 236 us -> 2.49 us
  starting transfers between devices: 203 us -> 0 us
  other arithmetic: 176 us -> 0.66 us
  matrix products: 116 us -> 0 us
  Pallas kernels: 0 us -> 94.9 us
  waiting for transfers between devices: 78.2 us -> 0 us
    another operation x2 -> x0, loops' own time: 430 us -> none  [body(): priors, transform = lax.fori_loop(0, values.shape[0], turn, start)]
    psum x2 -> x0, blocking collectives: 327 us -> none  [body(): priors, links = lax.psum((share, link_share), ('lon', 'lat'))]
    dynamic_slice x384 -> x0, local copies, waits for them, and re-layouts: 229 us -> none  [the longest x128 78.4 us: turn(): values[k]]
    ppermute x32 -> x0, starting transfers between devices: 203 us -> none  [the longest x16 147 us: with_halo(): lax.ppermute(head, axis, [((i + 1) % count, i) for i in range(count)])]
    reduce_sum x256 -> x0, other arithmetic: 152 us -> none  [the longest x128 76.5 us: increments(): jnp.sum(spread_dev * spread_dev) / (ensemble_snapshots - 1) + SMALL_EPSILON]
    dot_general x258 -> x0, matrix products: 116 us -> none  [the longest x128 95.4 us: turn(): lifted = jnp.dot(transform, slope, precision=lax.Precision.HIGHEST)]
    pallas_call x0 -> x2, Pallas kernels: none -> 94.9 us  [the longest x1 84.8 us: body(): pl.pallas_call(functools.partial(forecast_kernel, geo), out_shape=(jax.Sh...]
    ppermute x32 -> x0, waiting for transfers between devices: 78.2 us -> none  [the longest x16 70.2 us: with_halo(): lax.ppermute(head, axis, [((i + 1) % count, i) for i in range(count)])]
  transfers between devices with their start and end apart: 32 -> 0, of which waited for: 16 -> 0; matrix products, arithmetic and copies ran while one was open for 16% -> 0% of each run, Pallas kernels for 0% -> 0%
where the time goes in v1:
time: 99 us; the launch traced here: 98.1 us
  Pallas kernels  94.9 us (96%)
  local copies, waits for them, and re-layouts  2.49 us (3%)
    pallas_call x1, Pallas kernels, body(): pl.pallas_call(functools.partial(forecast_kernel, geo), out_shape=(jax.Sh...  84.8 us
    pallas_call x1, Pallas kernels, body(): pl.pallas_call(functools.partial(update_kernel, obs_cell.shape[1]), out_s...  10.1 us
    unnamed x11, local copies, waits for them, and re-layouts  2.36 us

profile of v1, /device:TPU:1, one launch (start us, length us, event | category | flops | bytes accessed | tf_op | source)
XLA Modules:
  0.0 98.1 jit_solution(6662383150116595762)
XLA Ops:
  0.0 0.0 copy-start.4
  0.0 0.5 broadcast.3
  0.5 0.2 copy-done.4
  0.7 0.7 reduce.3
  1.3 0.0 copy-start.1
  1.4 0.0 copy-start.2
  1.4 0.0 copy-start.3
  1.4 0.1 reshape.12.mask_ref
  1.5 0.5 copy-done.1
  2.0 0.0 copy-done.2
  2.0 0.0 copy-done.3
  2.1 0.0 copy-start
  2.1 1.1 %copy-done = f32[3,64,8,128]{3,2,1,0:T(8,128)S(1)} copy-done((f32[3,64,8,128]{3,2,1,0:T(8,128)S(1)}, f32[3,64,8,128]{3,2,1,0:T(8,128)}, u32[]{:S(2)}) %copy-start) | copy-done | bytes 786456
  3.2 84.8 %shard_map.55 = (f32[24,64,128]{2,1,0:T(8,128)S(1)}, f32[5,128,128]{2,1,0:T(8,128)S(1)}, f32[64,128]{1,0:T(8,128)S(1)}) custom-call(f32[3,512,128]{2,1,0:T(8,128)S(1)} %bitcast.3, s32[2,64]{1,0:T(2,128)S(1)} %copy-done.1, f32[2,64]{1,0:T(2,128)S(1)} %copy-done.2, f32[2,64]{1,0:T(2,128)S(1)} %copy-done.3, s32[128,1]{1,0:T(8,128)S(1)} %reshape.12.mask_ref), custom_call_target="tpu_custom_call" | custom-call | tf_op jit(solution)/shard_map/pallas_call | solution.py:480
  88.0 10.1 %shard_map.56 = f32[3,512,128]{2,1,0:T(8,128)} custom-call(f32[24,64,128]{2,1,0:T(8,128)S(1)} %get-tuple-element.8.f_ref, f32[5,128,128]{2,1,0:T(8,128)S(1)} %get-tuple-element.9.c_ref, f32[64,128]{1,0:T(8,128)S(1)} %get-tuple-element.10.y_ref), custom_call_target="tpu_custom_call" | custom-call | tf_op jit(solution)/shard_map/pallas_call | solution.py:505
Async XLA Ops:
  0.0 0.7 copy-start.4
  1.3 0.7 copy-start.1
  1.4 0.7 copy-start.2
  1.4 0.7 copy-start.3
  2.1 1.1 %copy-start = (f32[3,64,8,128]{3,2,1,0:T(8,128)S(1)}, f32[3,64,8,128]{3,2,1,0:T(8,128)}, u32[]{:S(2)}) copy-start(f32[3,64,8,128]{3,2,1,0:T(8,128)} %param.5) | copy-start | bytes 2359300

commit v2 on v1

v2 whole, which is shorter than its diff:
```python
import functools

import jax
import jax.numpy as jnp
from jax import lax
from jax.experimental import pallas as pl
from jax.experimental.pallas import tpu as pltpu
from jax.sharding import PartitionSpec as P

MESH = pl.DeviceIdType.MESH
F32 = jnp.float32
BF16 = jnp.bfloat16

STEPS = 4
LOC_RADIUS = 256
CORIOLIS = 0.1
SMALL_EPSILON = 1e-06
MEMBERS = 64
ROWS = 8
COLS = 128
GROUPS = 8
HALVES = 2 * STEPS
EXT = HALVES - 1
PICK_ROWS = ROWS + 2 * EXT


class Geometry:
    def __init__(self, n_lon, n_lat):
        self.n_lon, self.n_lat = n_lon, n_lat
        if (n_lon, n_lat) == (32, 32):
            self.x, self.y, self.zh, self.c = 4, 4, 4, 2
        else:
            self.x, self.y, self.zh, self.c = 1, 1, n_lat // 2, 2
        self.zl = n_lon // self.x
        self.near = self.x * self.y * self.c
        self.total_rows = ROWS * n_lat
        self.total_cols = COLS * n_lon

    def near_index(self, lon, lat):
        return (lon % self.x) * (self.y * self.c) + (lat // (self.zh * self.c)) * self.c + lat % self.c

    def near_peer(self, i, lon, lat):
        x, y, c = i // (self.y * self.c), (i // self.c) % self.y, i % self.c
        return (lon // self.x) * self.x + x, (y * self.zh + (lat // self.c) % self.zh) * self.c + c


def iota(shape, dim):
    return lax.broadcasted_iota(jnp.int32, shape, dim)


def roll(v, shift):
    return pltpu.roll(v, shift % COLS, 1)


def pack_edges(tiles):
    lane = iota((8, COLS), 1)
    out = None
    for s, t in enumerate(tiles):
        r = roll(t, 16 * s + 8)
        out = r if out is None else jnp.where(lane // 16 == s, r, out)
    return out


def unpack_edges(packed, s):
    return roll(packed, -(16 * s + 8))


def lon_diff(m, s, first, last):
    mp, sp, mm, sm = roll(m, -1), roll(s, -1), roll(m, 1), roll(s, 1)
    return (
        jnp.where(last, sp, mp) - jnp.where(first, sm, mm),
        jnp.where(last, mp, sp) - jnp.where(first, mm, sm),
    )


def column_of(row, eye):
    return jnp.sum(jnp.where(eye, row, 0.0), axis=1, keepdims=True)


class Sum:
    def __init__(self, geo, lon, lat, refs, sems):
        self.geo, self.lon, self.lat = geo, lon, lat
        self.src, self.near, self.mid, self.run, self.pair, self.pair_in, self.last, self.out = refs
        self.sems = sems
        self.me = geo.near_index(lon, lat)
        self.me_run = lon // geo.x

    def run_peer(self, i, lon, lat):
        return i * self.geo.x + lon % self.geo.x, lat

    def partner(self, step):
        geo, c = self.geo, self.geo.c
        zh = (self.lat // c) % geo.zh
        up = (zh + step) % 2 == 0
        other = jnp.where(up, zh + 1, zh + geo.zh - 1) % geo.zh
        return self.lon, ((self.lat // (geo.zh * c)) * geo.zh + other) * c + self.lat % c

    def _send(self, stage, src, dst, n, me, peer):
        def one(i, carry):
            p = lax.rem(me + i, n)
            pltpu.make_async_remote_copy(
                src_ref=src(p),
                dst_ref=dst.at[me],
                send_sem=self.sems.at[0, stage],
                recv_sem=self.sems.at[1, stage],
                device_id=peer(p, self.lon, self.lat),
                device_id_type=MESH,
            ).start()
            return carry

        lax.fori_loop(1, n, one, 0)

    def _wait(self, stage, buf, n, side=1):
        part = buf.at[pl.ds(0, n - 1)]
        pltpu.make_async_copy(part, part, self.sems.at[side, stage]).wait()

    def _added(self, buf, n):
        total = buf[0]
        for i in range(1, n):
            total = total + buf[i]
        return total

    def _pair_copy(self, step):
        return pltpu.make_async_remote_copy(
            src_ref=self.pair.at[step], dst_ref=self.pair_in.at[step], send_sem=self.sems.at[0, 2 + step],
            recv_sem=self.sems.at[1, 2 + step], device_id=self.partner(step), device_id_type=MESH,
        )

    def send_near(self):
        self.near[self.me] = self.src[self.me]
        self._send(0, lambda p: self.src.at[p], self.near, self.geo.near, self.me, self.geo.near_peer)

    def send_run(self):
        self._wait(0, self.near, self.geo.near)
        total = self._added(self.near, self.geo.near)
        self.mid[...] = total
        self.run[self.me_run] = total
        self._send(1, lambda p: self.mid, self.run, self.geo.zl, self.me_run, self.run_peer)

    def send_pair(self):
        self._wait(1, self.run, self.geo.zl)
        self.pair[0] = self._added(self.run, self.geo.zl)
        self._pair_copy(0).start()

    def send_pairs(self):
        self._pair_copy(0).wait_recv()
        self.pair[1] = self.pair[0] + self.pair_in[0]
        self._pair_copy(1).start()

    def send_last(self):
        self._pair_copy(1).wait_recv()
        total = self.pair[1] + self.pair_in[1]
        self.last[...] = total
        self.out[self.me] = total
        self._send(4, lambda p: self.last, self.out, self.geo.near, self.me, self.geo.near_peer)

    def wait_last(self):
        self._wait(4, self.out, self.geo.near)

    def wait_sends(self):
        for stage, buf, n in ((0, self.near, self.geo.near), (1, self.run, self.geo.zl), (4, self.out, self.geo.near)):
            self._wait(stage, buf, n, side=0)
        for step in range(2):
            self._pair_copy(step).wait_send()


def forecast_kernel(
    geo, x_hbm, cell_hbm, value_hbm, variance_hbm, mask_hbm,
    f_ref, c_ref, y_ref,
    x_ref, cell_ref, value_ref, variance_ref, mask_ref, main, side, edges, edges_in, series, series_in, late, late_in, ghosts, heights, onehot,
    s0, s1, s2, s3, s4, s5, s6, s7,
    in_sems, lon_sems, lat_sems, late_sems, sum_sems,
):
    lon, lat = lax.axis_index("lon"), lax.axis_index("lat")
    n_lon, n_lat = geo.n_lon, geo.n_lat
    east, west = lax.rem(lon + 1, n_lon), lax.rem(lon + n_lon - 1, n_lon)
    after, before = lax.rem(lat + 1, n_lat), lax.rem(lat + n_lat - 1, n_lat)
    shared = Sum(geo, lon, lat, (s0, s1, s2, s3, s4, s5, s6, s7), sum_sems)

    loads = [
        pltpu.make_async_copy(src, dst, in_sems.at[i])
        for i, (src, dst) in enumerate(
            (
                (x_hbm, x_ref), (cell_hbm, cell_ref), (value_hbm, value_ref), (variance_hbm, variance_ref), (mask_hbm, mask_ref),
            )
        )
    ]
    for load in loads:
        load.start()
    barrier = pltpu.get_barrier_semaphore()

    def greet(n, me, peer):
        def one(i, carry):
            pl.semaphore_signal(barrier, inc=1, device_id=peer(lax.rem(me + i, n), lon, lat), device_id_type=MESH)
            return carry

        lax.fori_loop(1, n, one, 0)

    for d in ((lon, after), (lon, before), shared.partner(0), shared.partner(1), (east, lat), (west, lat)):
        pl.semaphore_signal(barrier, inc=1, device_id=d, device_id_type=MESH)
    greet(geo.zl, shared.me_run, shared.run_peer)
    greet(geo.near, shared.me, geo.near_peer)

    row_first, col_first = lat * ROWS, lon * COLS
    lane = iota((8, COLS), 1)
    first, last = lane == 0, lane == COLS - 1
    edge = (lane < 8) | (lane >= COLS - 8)
    nothing = jnp.zeros((8, COLS), F32)
    has_before = jnp.where(lat > 0, 1.0, 0.0)
    has_after = jnp.where(lat < n_lat - 1, 1.0, 0.0)

    def field_row(f, g, r):
        return x_ref[f, pl.ds(g * 64 + r, 8, stride=8), :]

    def turning(r):
        row = (row_first + r).astype(F32)
        return CORIOLIS * ((2.0 * row + 1.0) / geo.total_rows - 1.0)

    def fit(r, v):
        return v * has_before if r < 0 else v * has_after if r >= ROWS else v

    class State:
        def __init__(self, g, own, sides):
            self.rows = [set(range(ROWS)) for _ in range(3)]
            for f in range(3):
                if sides:
                    packed = jnp.where(lane % 16 < 8, edges_in[0, g, f], edges_in[1, g, f])
                for r in range(ROWS):
                    main[f, r + 8] = field_row(f, g, r) if own else nothing
                    side[f, r + 8] = unpack_edges(packed, r) if sides else nothing

        def get(self, f, r):
            if r not in self.rows[f]:
                return None
            return main[f, r + 8], side[f, r + 8]

        def put(self, f, r, v):
            self.rows[f].add(r)
            main[f, r + 8], side[f, r + 8] = v

    def less(a, b):
        if a is None and b is None:
            return None
        if b is None:
            return a
        if a is None:
            return tuple(-q for q in b)
        return tuple(p - q for p, q in zip(a, b))

    def plus(a, b):
        if a is None or b is None:
            return a if b is None else b
        return tuple(p + q for p, q in zip(a, b))

    def scaled(a, k):
        return None if a is None else tuple(p * k for p in a)

    def lon_of(v):
        return None if v is None else lon_diff(v[0], v[1], first, last)

    def half_step(st, p, rows, ghost=None):
        at = (lambda f, r: ghost[r] if ghost is not None and r in ghost else st.get(f, r))
        for r in rows:
            if p % 2:
                slope = plus(lon_of(st.get(1, r)), less(at(2, r + 1), at(2, r - 1)))
                new = less(st.get(0, r), scaled(slope, 0.25))
                st.put(0, r, tuple(fit(r, v) for v in new))
            else:
                e, n, k = st.get(1, r), st.get(2, r), turning(r)
                new_e = less(plus(e, scaled(n, k)), scaled(lon_of(st.get(0, r)), 0.25))
                new_n = less(less(n, scaled(e, k)), scaled(less(at(0, r + 1), at(0, r - 1)), 0.25))
                if new_e is not None:
                    st.put(1, r, tuple(fit(r, v) for v in new_e))
                if new_n is not None:
                    st.put(2, r, tuple(fit(r, v) for v in new_n))

    beside = ((0, -1), (ROWS - 1, ROWS))

    def spread_tile(g, carry):
        for f in range(3):
            edges[g, f] = pack_edges([field_row(f, g, r) for r in range(ROWS)])
        st = State(g, True, False)
        sides = ([], [])
        for p in range(HALVES):
            if p > 0:
                half_step(st, p, range(-p, ROWS + p))
            f = 0 if p % 2 else 2
            for s, (r, outside) in enumerate(beside):
                m, e = st.get(f, r)
                series[s, g, p] = m
                sides[s].append(e)
                if p > 0:
                    ghosts[g, s, p, 0], ghosts[g, s, p, 1] = st.get(f, outside)
        for s in range(2):
            late[s, g, 0] = pack_edges(sides[s])
        here = pl.ds(pl.multiple_of(g * 8, 8), 8)
        for i in range(PICK_ROWS):
            heights[here, i * 128:(i + 1) * 128] = main[0, i - EXT + 8]
        for q in range(3):
            tiles = [side[0, i - EXT + 8] if i < PICK_ROWS else nothing for i in range(8 * q, 8 * q + 8)]
            heights[here, (PICK_ROWS + q) * 128:(PICK_ROWS + q + 1) * 128] = pack_edges(tiles)
        heights[here, (PICK_ROWS + 3) * 128:] = nothing
        return carry

    for load in loads:
        load.wait()
    lax.fori_loop(0, GROUPS, spread_tile, 0)

    big_row, big_col = iota((128, 128), 0), iota((128, 128), 1)
    eye = big_row == big_col
    cells = jnp.concatenate([cell_ref[0:1, :], cell_ref[1:2, :]], axis=1)
    obs_row, obs_col = cells // geo.total_cols, cells % geo.total_cols
    match_col = big_row + col_first == obs_col
    for i in range(PICK_ROWS):
        hit = match_col & (obs_row == row_first + (i - EXT))
        onehot[i * 128:(i + 1) * 128, :] = jnp.where(hit, 1.0, 0.0).astype(BF16)
    within = big_row % 16
    side_col = (jnp.where(within < 8, col_first - 8 + within, col_first + 120 + within) + geo.total_cols) % geo.total_cols
    match_col = side_col == obs_col
    for q in range(3):
        hit = match_col & (obs_row == row_first + (8 * q - EXT) + big_row // 16)
        i = PICK_ROWS + q
        onehot[i * 128:(i + 1) * 128, :] = jnp.where(hit, 1.0, 0.0).astype(BF16)
    onehot[(PICK_ROWS + 3) * 128:, :] = jnp.zeros((128, 128), BF16)
    total = jnp.zeros((3 * MEMBERS, 128), F32)
    for i in range((PICK_ROWS + 4) // 2):
        v = heights[:, i * 256:(i + 1) * 256]
        high = v.astype(BF16)
        rest = v - high.astype(F32)
        middle = rest.astype(BF16)
        low = (rest - middle.astype(F32)).astype(BF16)
        total = total + jnp.dot(
            jnp.concatenate([high, middle, low], axis=0), onehot[i * 256:(i + 1) * 256, :], preferred_element_type=F32
        )
    picked = total[:MEMBERS] + (total[MEMBERS:2 * MEMBERS] + total[2 * MEMBERS:])
    few, per = MEMBERS // geo.near, 128 // geo.near
    owned = jnp.where((obs_row // ROWS == lat) & (obs_col // COLS == lon), 1.0, 0.0)
    mask_row = jnp.concatenate([mask_ref[0], mask_ref[1]], axis=1).astype(F32)
    mask_col = column_of(mask_row, eye)
    share = mask_col * owned
    for i in range(geo.near):
        s0[i, 0:few, :] = picked[i * few:(i + 1) * few, :]
        s0[i, few:few + per, :] = share[i * per:(i + 1) * per, :]
        s0[i, few + per:, :] = jnp.zeros((s0.shape[1] - few - per, 128), F32)

    def lon_copies(g):
        return [
            pltpu.make_async_remote_copy(
                src_ref=edges.at[g], dst_ref=edges_in.at[s, g], send_sem=lon_sems.at[0, s, g], recv_sem=lon_sems.at[1, s, g],
                device_id=(d, lat), device_id_type=MESH,
            )
            for s, d in ((0, east), (1, west))
        ]

    def lat_copies(g, src, dst, sems):
        return [
            pltpu.make_async_remote_copy(
                src_ref=src.at[s, g], dst_ref=dst.at[1 - s, g], send_sem=sems.at[0, s, g],
                recv_sem=sems.at[1, 1 - s, g], device_id=(lon, d), device_id_type=MESH,
            )
            for s, d in ((0, before), (1, after))
        ]

    def series_copies(g):
        return lat_copies(g, series, series_in, lat_sems)

    def late_copies(g):
        return lat_copies(g, late, late_in, late_sems)

    def start(copies, lo, hi):
        def one(g, carry):
            for c in copies(g):
                c.start()
            return carry

        lax.fori_loop(lo, hi, one, 0)

    pl.semaphore_wait(barrier, 6 + (geo.zl - 1) + (geo.near - 1))
    shared.send_near()
    start(lon_copies, 0, GROUPS)
    start(series_copies, 0, 2)

    cells_col = column_of(cells.astype(F32), eye).astype(jnp.int32)
    row_col, col_col = cells_col // geo.total_cols, cells_col % geo.total_cols

    def damping(centre_row, centre_col):
        row_gap = row_col - centre_row
        col_gap = jnp.abs(col_col - centre_col)
        col_gap = jnp.minimum(col_gap, geo.total_cols - col_gap)
        distance = (row_gap * row_gap + col_gap * col_gap).astype(F32)
        return 1.0 + distance / (LOC_RADIUS * LOC_RADIUS)

    own = mask_col / damping(row_first + ROWS // 2, col_first + COLS // 2)
    value_col = column_of(jnp.concatenate([value_ref[0:1, :], value_ref[1:2, :]], axis=1), eye)
    variance_col = column_of(jnp.concatenate([variance_ref[0:1, :], variance_ref[1:2, :]], axis=1), eye)
    c_ref[1] = jnp.broadcast_to(1.0 / variance_col, (128, 128))
    c_ref[2] = jnp.broadcast_to(value_col, (128, 128))
    c_ref[3] = jnp.broadcast_to(own, (128, 128))

    shared.send_run()
    start(series_copies, 2, 4)

    def spread_sides(g, carry):
        for c in lon_copies(g):
            c.wait_recv()
        st = State(g, False, True)
        sides, mains = ([], []), ([], [])
        for p in range(HALVES):
            if p > 0:
                reach = EXT - p
                rows = [
                    r for r in range(-p, ROWS + p)
                    if -1 - reach <= r <= reach or ROWS - 1 - reach <= r <= ROWS + reach
                ]
                half_step(st, p, rows)
            f = 0 if p % 2 else 2
            for s, (r, outside) in enumerate(beside):
                m, e = st.get(f, r)
                mains[s].append(m)
                sides[s].append(e)
                if p > 0:
                    m, e = st.get(f, outside)
                    ghosts[g, s, p, 0] += m
                    ghosts[g, s, p, 1] += e
        for s in range(2):
            late[s, g, 0] += pack_edges(sides[s])
            late[s, g, 1] = pack_edges(mains[s])
        return carry

    def settle(g, carry):
        for c in series_copies(g) + late_copies(g):
            c.wait_recv()
        st = State(g, True, True)
        packed = [(late_in[s, g, 0], late_in[s, g, 1]) for s in range(2)]
        for p in range(1, HALVES + 1):
            ghost = {}
            for s, ((_, outside), there) in enumerate(zip(beside, (has_before, has_after))):
                m = series_in[s, g, p - 1] + jnp.where(edge, unpack_edges(packed[s][1], p - 1), 0.0)
                v = (m * there, unpack_edges(packed[s][0], p - 1) * there)
                if p > 1:
                    v = plus(v, (ghosts[g, s, p - 1, 0], ghosts[g, s, p - 1, 1]))
                ghost[outside] = v
            half_step(st, p, range(ROWS), ghost)
        for f in range(3):
            for r in range(ROWS):
                f_ref[f * ROWS + r, pl.ds(pl.multiple_of(g * 8, 8), 8), :] = main[f, r + 8]
        return carry

    lax.fori_loop(0, GROUPS, spread_sides, 0)
    shared.send_pair()
    start(late_copies, 0, 4)
    start(series_copies, 4, 7)
    shared.send_pairs()
    start(series_copies, 7, GROUPS)
    start(late_copies, 4, GROUPS)
    lax.fori_loop(0, 2, settle, 0)
    shared.send_last()

    lax.fori_loop(2, GROUPS, settle, 0)
    shared.wait_last()
    for i in range(geo.near):
        y_ref[i * few:(i + 1) * few, :] = s7[i, 0:few, :]
        c_ref[0, i * per:(i + 1) * per, :] = s7[i, few:few + per, :]
    weighted = c_ref[0] / damping(obs_row // ROWS * ROWS + ROWS // 2, obs_col // COLS * COLS + COLS // 2)
    c_ref[0] = weighted
    following = jnp.sum(jnp.where(big_col == big_row + 1, weighted, 0.0), axis=1, keepdims=True)
    c_ref[4] = jnp.broadcast_to(following, (128, 128))

    shared.wait_sends()

    def finish(g, carry):
        for c in lon_copies(g) + series_copies(g) + late_copies(g):
            c.wait_send()
        return carry

    lax.fori_loop(0, GROUPS, finish, 0)


def added_sublanes(v):
    t = v.reshape(8, 8, COLS).sum(axis=0)
    for s in (4, 2, 1):
        t = t + pltpu.roll(t, s, 0)
    return t


def tall(v):
    return jnp.concatenate([v] * 8, axis=0)


def across(column):
    return jnp.broadcast_to(column, (column.shape[0], COLS))


def update_kernel(n_obs, f_ref, c_ref, y_ref, out_ref):
    y = y_ref[...]
    mean = added_sublanes(y) * (1.0 / MEMBERS)
    b = y - tall(mean)
    a = jnp.where(iota((MEMBERS, COLS), 0) == iota((MEMBERS, COLS), 1), 1.0, 0.0)
    a_mean = jnp.zeros((8, COLS), F32)
    left = iota((8, COLS), 1) < MEMBERS

    def row(i, k):
        return jnp.broadcast_to(c_ref[i, k:k + 1, :], (8, COLS))

    d, m = across(b[:, 0:1]), across(mean[:, 0:1])
    for k in range(2 * n_obs):
        if k == n_obs:
            a, a_mean = jnp.where(tall(left), a, b), jnp.where(left, a_mean, mean)
        later = k >= n_obs
        obs, obs_mean = (a, a_mean) if later else (b, mean)
        if k + 1 < 2 * n_obs:
            d_next, m_next = across(obs[:, k + 1:k + 2]), across(obs_mean[:, k + 1:k + 2])
        s = added_sublanes(d * d) * (1.0 / (MEMBERS - 1)) + SMALL_EPSILON
        ratio = s * row(1, k)
        root = lax.rsqrt(1.0 + ratio)
        gain = root - 1.0
        shift = ratio * (root * root) * (row(2, k) - m)
        scale = 1.0 / ((MEMBERS - 1) * s)
        if k + 1 < 2 * n_obs:
            c = row(4, k) * scale * added_sublanes(d_next * d)
            new_d, new_m = d_next + tall(c * gain) * d, m_next + c * shift
        link, own = row(0, k), row(3, k)
        c = (jnp.where(left, own, link) if later else own) * scale * added_sublanes(a * d)
        a, a_mean = a + tall(c * gain) * d, a_mean + c * shift
        if not later:
            c = link * scale * added_sublanes(b * d)
            b, mean = b + tall(c * gain) * d, mean + c * shift
        if k + 1 < 2 * n_obs:
            d, m = new_d, new_m
    t = (a + tall(a_mean))[:, :MEMBERS]
    t_high = t.astype(BF16)
    t_low = (t - t_high.astype(F32)).astype(BF16)
    lhs = jnp.concatenate([t_high, t_high, t_low, t_low], axis=1)
    for i in range(0, 3 * ROWS, 2):
        v = jnp.concatenate([f_ref[i], f_ref[i + 1]], axis=1)
        high = v.astype(BF16)
        low = (v - high.astype(F32)).astype(BF16)
        r = jnp.dot(lhs, jnp.concatenate([high, low, high, low], axis=0), preferred_element_type=F32)
        for q in range(2):
            out_ref[(i + q) // ROWS, pl.ds((i + q) % ROWS, MEMBERS, stride=ROWS), :] = r[:, q * COLS:(q + 1) * COLS]


def body(geo, model_variables, obs_cell, obs_value, obs_variance, tile_mask):
    vmem = pl.BlockSpec(memory_space=pltpu.VMEM)
    x = model_variables.reshape(3, MEMBERS * ROWS, COLS)
    mask = jnp.transpose(tile_mask, (0, 2, 1))
    n, rows = geo.near, -(-(MEMBERS + 128) // geo.near // 8) * 8
    dma = pltpu.SemaphoreType.DMA

    def v(*shape, dtype=F32):
        return pltpu.VMEM(shape, dtype)

    f, c, y = pl.pallas_call(
        functools.partial(forecast_kernel, geo),
        out_shape=(
            jax.ShapeDtypeStruct((3 * ROWS, MEMBERS, COLS), F32),
            jax.ShapeDtypeStruct((5, 128, 128), F32),
            jax.ShapeDtypeStruct((MEMBERS, 128), F32),
        ),
        in_specs=[pl.BlockSpec(memory_space=pltpu.HBM)] * 5,
        out_specs=(vmem, vmem, vmem),
        scratch_shapes=[
            v(3, MEMBERS * ROWS, COLS),
            v(*obs_cell.shape, dtype=jnp.int32), v(*obs_value.shape), v(*obs_value.shape), v(*mask.shape, dtype=jnp.int32),
            v(3, 24, 8, COLS),
            v(3, 24, 8, COLS),
            v(GROUPS, 3, 8, COLS),
            v(2, GROUPS, 3, 8, COLS),
            v(2, GROUPS, HALVES, 8, COLS),
            v(2, GROUPS, HALVES, 8, COLS),
            v(2, GROUPS, 2, 8, COLS),
            v(2, GROUPS, 2, 8, COLS),
            v(GROUPS, 2, HALVES, 2, 8, COLS),
            v(MEMBERS, (PICK_ROWS + 4) * COLS),
            v((PICK_ROWS + 4) * COLS, 128, dtype=BF16),
            v(n, rows, 128), v(n, rows, 128), v(rows, 128), v(geo.zl, rows, 128), v(2, rows, 128), v(2, rows, 128), v(rows, 128),
            v(n, rows, 128),
            dma((5,)), dma((2, 2, GROUPS)), dma((2, 2, GROUPS)), dma((2, 2, GROUPS)), dma((2, 5)),
        ],
        compiler_params=pltpu.CompilerParams(collective_id=0, has_side_effects=True, vmem_limit_bytes=40 * 2**20),
    )(x, obs_cell, obs_value, obs_variance, mask)
    out = pl.pallas_call(
        functools.partial(update_kernel, obs_cell.shape[1]),
        out_shape=jax.ShapeDtypeStruct((3, MEMBERS * ROWS, COLS), F32),
        in_specs=[vmem] * 3,
        out_specs=vmem,
        compiler_params=pltpu.CompilerParams(vmem_limit_bytes=32 * 2**20),
    )(f, c, y)
    return out.reshape(3, MEMBERS, ROWS, COLS)


def solution(mesh):
    geo = Geometry(mesh.shape["lon"], mesh.shape["lat"])
    in_specs = (P(None, None, "lat", "lon"), P(), P(), P(), P(None, None, ("lon", "lat")))
    out_specs = P(None, None, "lat", "lon")
    return jax.shard_map(
        functools.partial(body, geo), mesh=mesh, in_specs=in_specs, out_specs=out_specs, check_vma=False
    )
```

time: 99 us -> 90 us (0.909)
  Pallas kernels: 94.9 us -> 87.2 us
    pallas_call x1, Pallas kernels: 84.8 us -> 77.1 us  [body(): pl.pallas_call(functools.partial(forecast_kernel, geo), out_shape=(jax.Sh...]
    unnamed x11 -> x10, local copies, waits for them, and re-layouts: 2.36 us -> 2.52 us
where the time goes in v2:
time: 90 us; the launch traced here: 89.7 us
  Pallas kernels  87.2 us (97%)
  local copies, waits for them, and re-layouts  2.52 us (3%)
    pallas_call x1, Pallas kernels, body(): pl.pallas_call(functools.partial(forecast_kernel, geo), out_shape=(jax.Sh...  77.1 us
    pallas_call x1, Pallas kernels, body(): pl.pallas_call(functools.partial(update_kernel, obs_cell.shape[1]), out_s...  10.1 us
    unnamed x10, local copies, waits for them, and re-layouts  2.52 us

profile of v2, /device:TPU:1, one launch (start us, length us, event | category | flops | bytes accessed | tf_op | source)
XLA Modules:
  0.0 89.7 jit_solution(14765079901164956888)
XLA Ops:
  0.0 0.0 copy-start.2
  0.0 0.0 copy-start.3
  0.0 0.0 copy-start.1
  0.0 0.7 copy-done.2
  0.7 0.0 copy-done.3
  0.7 0.0 copy-done.1
  0.7 0.0 copy-start
  0.7 1.1 %copy-done = f32[3,64,8,128]{3,2,1,0:T(8,128)S(1)} copy-done((f32[3,64,8,128]{3,2,1,0:T(8,128)S(1)}, f32[3,64,8,128]{3,2,1,0:T(8,128)}, u32[]{:S(2)}) %copy-start) | copy-done | bytes 786456
  1.8 0.0 copy-start.4
  1.8 0.7 copy-done.4
  2.5 77.1 %shard_map.55 = (f32[24,64,128]{2,1,0:T(8,128)S(1)}, f32[5,128,128]{2,1,0:T(8,128)S(1)}, f32[64,128]{1,0:T(8,128)S(1)}) custom-call(f32[3,512,128]{2,1,0:T(8,128)S(1)} %bitcast.5, s32[2,64]{1,0:T(2,128)S(1)} %copy-done.1, f32[2,64]{1,0:T(2,128)S(1)} %copy-done.2, f32[2,64]{1,0:T(2,128)S(1)} %copy-done.3, s32[2,1,64]{2,1,0:T(1,128)S(1)} %bitcast.6), custom_call_target="tpu_custom_call" | custom-call | tf_op jit(solution)/shard_map/pallas_call | solution.py:553
  79.7 10.1 %shard_map.56 = f32[3,512,128]{2,1,0:T(8,128)} custom-call(f32[24,64,128]{2,1,0:T(8,128)S(1)} %get-tuple-element.8.f_ref, f32[5,128,128]{2,1,0:T(8,128)S(1)} %get-tuple-element.9.c_ref, f32[64,128]{1,0:T(8,128)S(1)} %get-tuple-element.10.y_ref), custom_call_target="tpu_custom_call" | custom-call | tf_op jit(solution)/shard_map/pallas_call | solution.py:582
Async XLA Ops:
  0.0 0.7 copy-start.2
  0.0 0.7 copy-start.3
  0.0 0.7 copy-start.1
  0.7 1.1 %copy-start = (f32[3,64,8,128]{3,2,1,0:T(8,128)S(1)}, f32[3,64,8,128]{3,2,1,0:T(8,128)}, u32[]{:S(2)}) copy-start(f32[3,64,8,128]{3,2,1,0:T(8,128)} %param.5) | copy-start | bytes 2359300
  1.8 0.7 copy-start.4

commit v3 on v2

--- a/solution.py
+++ b/solution.py
@@ -390,6 +390,7 @@
         distance = (row_gap * row_gap + col_gap * col_gap).astype(F32)
         return 1.0 + distance / (LOC_RADIUS * LOC_RADIUS)
 
+    c_ref[0] = damping(obs_row // ROWS * ROWS + ROWS // 2, obs_col // COLS * COLS + COLS // 2)
     own = mask_col / damping(row_first + ROWS // 2, col_first + COLS // 2)
     value_col = column_of(jnp.concatenate([value_ref[0:1, :], value_ref[1:2, :]], axis=1), eye)
     variance_col = column_of(jnp.concatenate([variance_ref[0:1, :], variance_ref[1:2, :]], axis=1), eye)
@@ -446,12 +447,13 @@
                 f_ref[f * ROWS + r, pl.ds(pl.multiple_of(g * 8, 8), 8), :] = main[f, r + 8]
         return carry
 
-    lax.fori_loop(0, GROUPS, spread_sides, 0)
+    lax.fori_loop(0, 5, spread_sides, 0)
     shared.send_pair()
+    start(series_copies, 4, 6)
+    lax.fori_loop(5, GROUPS, spread_sides, 0)
     start(late_copies, 0, 4)
-    start(series_copies, 4, 7)
     shared.send_pairs()
-    start(series_copies, 7, GROUPS)
+    start(series_copies, 6, GROUPS)
     start(late_copies, 4, GROUPS)
     lax.fori_loop(0, 2, settle, 0)
     shared.send_last()
@@ -460,9 +462,9 @@
     shared.wait_last()
     for i in range(geo.near):
         y_ref[i * few:(i + 1) * few, :] = s7[i, 0:few, :]
-        c_ref[0, i * per:(i + 1) * per, :] = s7[i, few:few + per, :]
-    weighted = c_ref[0] / damping(obs_row // ROWS * ROWS + ROWS // 2, obs_col // COLS * COLS + COLS // 2)
-    c_ref[0] = weighted
+        here = slice(i * per, (i + 1) * per)
+        c_ref[0, here, :] = s7[i, few:few + per, :] / c_ref[0, here, :]
+    weighted = c_ref[0]
     following = jnp.sum(jnp.where(big_col == big_row + 1, weighted, 0.0), axis=1, keepdims=True)
     c_ref[4] = jnp.broadcast_to(following, (128, 128))
 

time: 90 us -> 86.1 us (0.957)
  Pallas kernels: 87.2 us -> 83.3 us
    pallas_call x1, Pallas kernels: 77.1 us -> 73.3 us  [body(): pl.pallas_call(functools.partial(forecast_kernel, geo), out_shape=(jax.Sh...]
where the time goes in v3:
time: 86.1 us; the launch traced here: 85.9 us
  Pallas kernels  83.3 us (97%)
  local copies, waits for them, and re-layouts  2.52 us (3%)
    pallas_call x1, Pallas kernels, body(): pl.pallas_call(functools.partial(forecast_kernel, geo), out_shape=(jax.Sh...  73.3 us
    pallas_call x1, Pallas kernels, body(): pl.pallas_call(functools.partial(update_kernel, obs_cell.shape[1]), out_s...  10.1 us
    unnamed x10, local copies, waits for them, and re-layouts  2.52 us

profile of v3, /device:TPU:1, one launch (start us, length us, event | category | flops | bytes accessed | tf_op | source)
XLA Modules:
  0.0 85.9 jit_solution(7111323308652362103)
XLA Ops:
  0.0 0.0 copy-start.2
  0.0 0.0 copy-start.3
  0.0 0.0 copy-start.1
  0.0 0.7 copy-done.2
  0.7 0.0 copy-done.3
  0.7 0.0 copy-done.1
  0.7 0.0 copy-start
  0.7 1.1 %copy-done = f32[3,64,8,128]{3,2,1,0:T(8,128)S(1)} copy-done((f32[3,64,8,128]{3,2,1,0:T(8,128)S(1)}, f32[3,64,8,128]{3,2,1,0:T(8,128)}, u32[]{:S(2)}) %copy-start) | copy-done | bytes 786456
  1.8 0.0 copy-start.4
  1.8 0.7 copy-done.4
  2.5 73.3 %shard_map.55 = (f32[24,64,128]{2,1,0:T(8,128)S(1)}, f32[5,128,128]{2,1,0:T(8,128)S(1)}, f32[64,128]{1,0:T(8,128)S(1)}) custom-call(f32[3,512,128]{2,1,0:T(8,128)S(1)} %bitcast.5, s32[2,64]{1,0:T(2,128)S(1)} %copy-done.1, f32[2,64]{1,0:T(2,128)S(1)} %copy-done.2, f32[2,64]{1,0:T(2,128)S(1)} %copy-done.3, s32[2,1,64]{2,1,0:T(1,128)S(1)} %bitcast.6), custom_call_target="tpu_custom_call" | custom-call | tf_op jit(solution)/shard_map/pallas_call | solution.py:555
  75.8 10.1 %shard_map.56 = f32[3,512,128]{2,1,0:T(8,128)} custom-call(f32[24,64,128]{2,1,0:T(8,128)S(1)} %get-tuple-element.8.f_ref, f32[5,128,128]{2,1,0:T(8,128)S(1)} %get-tuple-element.9.c_ref, f32[64,128]{1,0:T(8,128)S(1)} %get-tuple-element.10.y_ref), custom_call_target="tpu_custom_call" | custom-call | tf_op jit(solution)/shard_map/pallas_call | solution.py:584
Async XLA Ops:
  0.0 0.7 copy-start.2
  0.0 0.7 copy-start.3
  0.0 0.7 copy-start.1
  0.7 1.1 %copy-start = (f32[3,64,8,128]{3,2,1,0:T(8,128)S(1)}, f32[3,64,8,128]{3,2,1,0:T(8,128)}, u32[]{:S(2)}) copy-start(f32[3,64,8,128]{3,2,1,0:T(8,128)} %param.5) | copy-start | bytes 2359300
  1.8 0.7 copy-start.4

commit v4 on v3

--- a/solution.py
+++ b/solution.py
@@ -380,6 +380,9 @@
     start(lon_copies, 0, GROUPS)
     start(series_copies, 0, 2)
 
+    shared.send_run()
+    start(series_copies, 2, 4)
+
     cells_col = column_of(cells.astype(F32), eye).astype(jnp.int32)
     row_col, col_col = cells_col // geo.total_cols, cells_col % geo.total_cols
 
@@ -397,9 +400,6 @@
     c_ref[1] = jnp.broadcast_to(1.0 / variance_col, (128, 128))
     c_ref[2] = jnp.broadcast_to(value_col, (128, 128))
     c_ref[3] = jnp.broadcast_to(own, (128, 128))
-
-    shared.send_run()
-    start(series_copies, 2, 4)
 
     def spread_sides(g, carry):
         for c in lon_copies(g):

time: 86.1 us -> 86.1 us (level)
  no operation moved by 1% of the time
where the time goes in v4:
time: 86.1 us; the launch traced here: 85.9 us
  Pallas kernels  83.3 us (97%)
  local copies, waits for them, and re-layouts  2.52 us (3%)
    pallas_call x1, Pallas kernels, body(): pl.pallas_call(functools.partial(forecast_kernel, geo), out_shape=(jax.Sh...  73.3 us
    pallas_call x1, Pallas kernels, body(): pl.pallas_call(functools.partial(update_kernel, obs_cell.shape[1]), out_s...  10.1 us
    unnamed x10, local copies, waits for them, and re-layouts  2.52 us

profile of v4, /device:TPU:1, one launch (start us, length us, event | category | flops | bytes accessed | tf_op | source)
XLA Modules:
  0.0 85.9 jit_solution(3567828845379867301)
XLA Ops:
  0.0 0.0 copy-start.2
  0.0 0.0 copy-start.3
  0.0 0.0 copy-start.1
  0.0 0.7 copy-done.2
  0.7 0.0 copy-done.3
  0.7 0.0 copy-done.1
  0.7 0.0 copy-start
  0.7 1.1 %copy-done = f32[3,64,8,128]{3,2,1,0:T(8,128)S(1)} copy-done((f32[3,64,8,128]{3,2,1,0:T(8,128)S(1)}, f32[3,64,8,128]{3,2,1,0:T(8,128)}, u32[]{:S(2)}) %copy-start) | copy-done | bytes 786456
  1.8 0.0 copy-start.4
  1.8 0.7 copy-done.4
  2.5 73.3 %shard_map.55 = (f32[24,64,128]{2,1,0:T(8,128)S(1)}, f32[5,128,128]{2,1,0:T(8,128)S(1)}, f32[64,128]{1,0:T(8,128)S(1)}) custom-call(f32[3,512,128]{2,1,0:T(8,128)S(1)} %bitcast.5, s32[2,64]{1,0:T(2,128)S(1)} %copy-done.1, f32[2,64]{1,0:T(2,128)S(1)} %copy-done.2, f32[2,64]{1,0:T(2,128)S(1)} %copy-done.3, s32[2,1,64]{2,1,0:T(1,128)S(1)} %bitcast.6), custom_call_target="tpu_custom_call" | custom-call | tf_op jit(solution)/shard_map/pallas_call | solution.py:555
  75.8 10.1 %shard_map.56 = f32[3,512,128]{2,1,0:T(8,128)} custom-call(f32[24,64,128]{2,1,0:T(8,128)S(1)} %get-tuple-element.8.f_ref, f32[5,128,128]{2,1,0:T(8,128)S(1)} %get-tuple-element.9.c_ref, f32[64,128]{1,0:T(8,128)S(1)} %get-tuple-element.10.y_ref), custom_call_target="tpu_custom_call" | custom-call | tf_op jit(solution)/shard_map/pallas_call | solution.py:584
Async XLA Ops:
  0.0 0.7 copy-start.2
  0.0 0.7 copy-start.3
  0.0 0.7 copy-start.1
  0.7 1.1 %copy-start = (f32[3,64,8,128]{3,2,1,0:T(8,128)S(1)}, f32[3,64,8,128]{3,2,1,0:T(8,128)}, u32[]{:S(2)}) copy-start(f32[3,64,8,128]{3,2,1,0:T(8,128)} %param.5) | copy-start | bytes 2359300
  1.8 0.7 copy-start.4
